TPU v7x, 256 devices: a whole 4x4x8 slice. The times are simulated.
256 devices in a mesh: blk: 128 (over z_hi, y, x, core), head: 2 (over z_lo).
Axes of the slice: x: 4, y: 4, z: 8 (z_hi: 4, z_lo: 2; z = z_hi * 2 + z_lo), core: 2. Of those that a mesh axis runs over, the one named last changes fastest.
Arguments:
- cells: bfloat16 [65536, 256], P('blk', 'head'), may hold values from -6 to 6
- w_query: bfloat16 [256, 256], P(None, 'head'), may hold values from -0.375 to 0.375
- w_key: bfloat16 [256, 256], P(None, 'head'), may hold values from -0.375 to 0.375
- w_value: bfloat16 [256, 256], P(None, 'head'), may hold values from -0.375 to 0.375
- w_source: bfloat16 [2, 256, 256], P(None, None, 'head'), may hold values from -0.375 to 0.375
- w_target: bfloat16 [2, 256, 256], P(None, None, 'head'), may hold values from -0.375 to 0.375
- msg_bias: float32 [2, 256], P(None, 'head'), may hold values from -3 to 3
- w_out: bfloat16 [256, 256], P('head'), may hold values from -0.375 to 0.375
- nbr_block: int32 [512, 4], P('blk'), may hold values from 0 to 511, as said below
- edge_src: int32 [65536, 8], P('blk'), may hold values from 0 to 511
- key_blocks: int32 [512, 32], P('blk'), may hold values from 0 to 511, as said below
Outputs:
- updated: bfloat16 [65536, 256], P('blk', 'head')
Inputs may be any that keep to these rules, and one draw needn't show every extreme that they name: `nbr_block`: the source blocks listed for a destination block lie in its own partition of 4 consecutive blocks or in the partition just before or after it on the loop of 128 partitions. `key_blocks`: each row lists 32 key blocks from 32 different partitions; among all key blocks listed by the 4 query blocks of one partition, those that lie in one partition are the same block.
All inputs are finite; a program needn't handle non-finite values.
Results may differ from a plain program's by a relative error of at most 0.0015.
The roundings to bfloat16 on the way count: a program that leaves them out, or rounds other values in their place, can miss the bound.
Values may be sent and summed in bfloat16 or wider, within the bound.
No kernel may reach another device: no remote copies, remote signals or barrier semaphores. Data moves between devices by JAX's collectives and lax.ppermute only.
A program may use at most 128 MiB of HBM per device.

v0:
```python
import jax
import jax.numpy as jnp
from jax import lax
from jax.sharding import PartitionSpec as P

HEAD_DIM = 32
BLOCK = 128


def padded(value, sides, width):
    for axis, dim in sides:
        peers, length = (lax.axis_size(axis), value.shape[dim])
        up = [(i, (i + 1) % peers) for i in range(peers)]
        down = [(j, i) for i, j in up]
        last = lax.slice_in_dim(value, length - width, length, axis=dim)
        initial = lax.slice_in_dim(value, 0, width, axis=dim)
        before = lax.ppermute(last, axis, up)
        after = lax.ppermute(initial, axis, down)
        value = jnp.concatenate([before, value, after], axis=dim)
    return value


def body(
    cells,
    w_query,
    w_key,
    w_value,
    w_source,
    w_target,
    msg_bias,
    w_out,
    nbr_block,
    edge_src,
    key_blocks,
):
    rows = cells.shape[0]
    width = w_query.shape[1]
    heads_here = width // HEAD_DIM
    blk_dev = rows // BLOCK
    nparts = lax.axis_size("blk")
    edge_count = edge_src.shape[1]
    scale = HEAD_DIM ** (-0.5)
    whole = lax.all_gather(cells, "head", axis=1, tiled=True)
    queries = jnp.dot(whole, w_query, preferred_element_type=jnp.float32).astype(jnp.bfloat16)
    keys = jnp.dot(whole, w_key, preferred_element_type=jnp.float32).astype(jnp.bfloat16)
    values = jnp.dot(whole, w_value, preferred_element_type=jnp.float32).astype(jnp.bfloat16)
    source = jnp.einsum("cd,gdk->cgk", whole, w_source, preferred_element_type=jnp.float32)
    source = source.astype(jnp.bfloat16).reshape(rows, 2 * width)
    target = (
        jnp.einsum("cd,gdk->cgk", whole, w_target, preferred_element_type=jnp.float32)
        + msg_bias[None]
    )
    window = padded(source, (("blk", 0),), rows)
    mine = lax.axis_index("blk")
    own_block = jnp.arange(rows, dtype=jnp.int32) // BLOCK
    src_block = nbr_block[own_block[:, None], edge_src // BLOCK]
    offset = (src_block // blk_dev - mine + 1) % nparts
    window_row = offset * rows + src_block % blk_dev * BLOCK + edge_src % BLOCK
    fetched = jnp.take(window, window_row.reshape(-1), axis=0).reshape(rows, edge_count, 2, width)
    pre = fetched.astype(jnp.float32) + target[:, None]
    message = jax.nn.sigmoid(pre[:, :, 0]) * jax.nn.silu(pre[:, :, 1])
    aggregate = jnp.mean(message, axis=1)
    query_heads = queries.reshape(rows, heads_here, HEAD_DIM)
    part_of = key_blocks // blk_dev
    local_of = key_blocks % blk_dev

    def tile(carry, key_piece, value_piece, first):
        source_part = first // rows
        hit = part_of == source_part
        chosen_local = jnp.max(jnp.where(hit, local_of, -1))
        query_uses = jnp.any(hit, axis=1)
        numer, total = carry
        begin = jnp.maximum(chosen_local, 0) * BLOCK
        block_keys = lax.dynamic_slice_in_dim(key_piece, begin, BLOCK, 0)
        block_values = lax.dynamic_slice_in_dim(value_piece, begin, BLOCK, 0)
        row_mask = jnp.repeat(query_uses, BLOCK).astype(jnp.float32)
        scores = (
            jnp.einsum(
                "qhd,khd->hqk",
                query_heads,
                block_keys.reshape(BLOCK, heads_here, HEAD_DIM),
                preferred_element_type=jnp.float32,
            )
            * scale
        )
        weight = jnp.exp(scores) * row_mask[None, :, None]
        total = total + jnp.sum(weight, axis=2)
        added = jnp.einsum(
            "hqk,khd->qhd",
            weight.astype(jnp.bfloat16),
            block_values.reshape(BLOCK, heads_here, HEAD_DIM),
            preferred_element_type=jnp.float32,
        )
        return (numer + added.reshape(rows, width), total)

    initial = (jnp.zeros((rows, width), jnp.float32), jnp.zeros((heads_here, rows), jnp.float32))
    carry = initial
    key_piece = lax.all_gather(keys, "blk", axis=0, tiled=True)
    value_piece = lax.all_gather(values, "blk", axis=0, tiled=True)
    count = key_piece.shape[0]

    def advance(state, turn):
        first = turn * rows
        part_keys = lax.dynamic_slice_in_dim(key_piece, first, rows, 0)
        part_values = lax.dynamic_slice_in_dim(value_piece, first, rows, 0)
        return (tile(state, part_keys, part_values, first), None)

    carry, unused = lax.scan(advance, carry, jnp.arange(count // rows, dtype=jnp.int32))
    numer, total = carry
    mixed = (numer / jnp.repeat(jnp.transpose(total), HEAD_DIM, axis=1)).astype(jnp.bfloat16)
    partial_out = jnp.dot(mixed, w_out, preferred_element_type=jnp.float32)
    attended = lax.psum_scatter(partial_out, "head", scatter_dimension=1, tiled=True)
    return (cells.astype(jnp.float32) + aggregate + attended).astype(jnp.bfloat16)


def solution(mesh):
    in_specs = (
        P("blk", "head"),
        P(None, "head"),
        P(None, "head"),
        P(None, "head"),
        P(None, None, "head"),
        P(None, None, "head"),
        P(None, "head"),
        P("head", None),
        P("blk", None),
        P("blk", None),
        P("blk", None),
    )
    out_specs = P("blk", "head")
    return jax.shard_map(body, mesh=mesh, in_specs=in_specs, out_specs=out_specs, check_vma=False)
```

profile of v0, /device:TPU:1, one launch (start us, length us, event | category | flops | bytes accessed | tf_op | source)
XLA Modules:
  0.0 1106.5 jit_solution(5081986127554945908)
XLA Ops:
  6.5 5.9 all_gather.9
  12.4 1.7 convolution_convert_fusion.2
  14.2 1.7 convolution_convert_fusion.1
  17.5 3.3 collective-permute-start
  21.6 34.6 %gather_fusion = s32[4096]{0:T(1024)S(1)} fusion(s32[4,4]{1,0:T(4,128)S(1)} %copy-done.1, s32[4096]{0:T(1024)S(1)} %reshape.116), kind=kCustom, calls=%fused_computation | custom fusion | bytes 65536 | tf_op jit(solution)/shard_map/gather | solution.py:56
  59.5 14.6 %gather_fusion.1 = bf16[4096,256]{1,0:T(8,128)(2,1)S(1)} fusion(bf16[1536,256]{1,0:T(8,128)(2,1)S(1)} %pad_maximum_fusion, s32[4096]{0:T(1024)S(1)} %broadcast_clamp_fusion), kind=kCustom, calls=%fused_computation.1 | custom fusion | bytes 4210688 | tf_op jit(solution)/shard_map/jit(_take)/gather | solution.py:59
  74.1 54.5 %all-gather.3.cloned.1.call-done = bf16[65536,128]{1,0:T(8,128)(2,1)} async-done(((bf16[512,128]{1,0:T(8,128)(2,1)}), bf16[65536,128]{1,0:T(8,128)(2,1)}) %all-gather.3.cloned.1.call-update) | async-done | bytes 16777232 | tf_op jit(solution)/shard_map/all_gather | solution.py:99
  128.6 118.2 %all-gather.5.cloned.1.call-done = bf16[65536,128]{1,0:T(8,128)(2,1)} async-done(((bf16[512,128]{1,0:T(8,128)(2,1)}), bf16[65536,128]{1,0:T(8,128)(2,1)}) %all-gather.5.cloned.1.call-update) | async-done | bytes 16777232 | tf_op jit(solution)/shard_map/all_gather | solution.py:98
  247.3 824.6 %while.15 = (s32[]{:T(128)}, f32[512,128]{0,1:T(8,128)S(1)}, f32[4,512]{1,0:T(4,128)S(1)}, s32[128]{0:T(128)}, s32[4,32]{1,0:T(4,128)}, /*index=5*/s32[4,32]{1,0...) while((s32[]{:T(128)}, f32[512,128]{0,1:T(8,128)S(1)}, ...), condition=%wide.region_5.6_spmd.clone, body=%wide.region_1.5_spmd.clone.sunk | while | flops 34736664 | bytes 2594593 | solution.py:108
  249.9 1.3 select_reduce_fusion.2
  256.4 1.3 select_reduce_fusion.2
  269.3 1.3 select_reduce_fusion.2
  275.7 1.3 select_reduce_fusion.2
  282.1 1.3 select_reduce_fusion.2
  288.6 1.3 select_reduce_fusion.2
  295.0 1.3 select_reduce_fusion.2
  301.5 1.3 select_reduce_fusion.2
  307.9 1.3 select_reduce_fusion.2
  314.4 1.3 select_reduce_fusion.2
  1072.0 1.9 fusion.38
  1073.9 2.5 convert_add_fusion
  1076.4 1.9 fusion.11
  1078.4 19.9 %reduce-scatter.2.cloned.1.call-done = f32[512,128]{1,0:T(8,128)} async-done(((f32[512,256]{1,0:T(8,128)}), f32[512,128]{1,0:T(8,128)}) %reduce-scatter.2.cloned.1.call-update) | async-done | bytes 262160 | tf_op jit(solution)/shard_map/reduce_scatter | solution.py:112
  1098.3 1.7 add_convert_fusion
  (1571 shorter events, 653.7 us)
Async XLA Ops:
  6.5 50.6 %copy-start = (bf16[2,256,128]{2,1,0:T(8,128)(2,1)S(1)}, bf16[2,256,128]{2,1,0:T(8,128)(2,1)}, u32[]{:S(2)}) copy-start(bf16[2,256,128]{2,1,0:T(8,128)(2,1)} %param.18) | copy-start | bytes 393220
  6.5 14.5 %copy-start.4 = (s32[512,8]{0,1:T(8,128)S(1)}, s32[512,8]{0,1:T(8,128)}, u32[]{:S(2)}) copy-start(s32[512,8]{0,1:T(8,128)} %param.22) | copy-start | bytes 49156
  6.5 122.1 %all-gather.3.cloned.1.call-start = ((), (), s32[]{:S(2)}) async-start(), calls=%async_computation.1 | async-start | bytes 16908288 | tf_op jit(solution)/shard_map/all_gather | solution.py:99
  14.2 7.4 copy-start.1
  14.2 232.6 %all-gather.5.cloned.1.call-start = ((), (), s32[]{:S(2)}) async-start(), calls=%async_computation.2 | async-start | bytes 16908288 | tf_op jit(solution)/shard_map/all_gather | solution.py:98
  16.0 1082.3 %reduce-scatter.2.cloned.1.call-start = ((), (), s32[]{:S(2)}) async-start(), calls=%async_computation.3 | async-start | bytes 786432 | tf_op jit(solution)/shard_map/reduce_scatter | solution.py:112
  17.5 41.9 %collective-permute-start = (bf16[512,256]{1,0:T(8,128)(2,1)S(1)}, bf16[512,256]{1,0:T(8,128)(2,1)S(1)}, u32[]{:S(2)}, u32[]{:S(2)}) collective-permute-start(bf16[512,256]{1,0:T(8,128)(2,1)S(1)} %copy.28), channel_id=1, source_target_pairs={{0,2},{2,4},{4,6},{6,8},{8,10},{10,12},{12,14},{14,16},{16,18},{18... | collective-permute-start | bytes 786440 | tf_op jit(solution)/shard_map/ppermute | solution.py:17
  20.8 38.7 %collective-permute-start.1 = (bf16[512,256]{1,0:T(8,128)(2,1)S(1)}, bf16[512,256]{1,0:T(8,128)(2,1)S(1)}, u32[]{:S(2)}, u32[]{:S(2)}) collective-permute-start(bf16[512,256]{1,0:T(8,128)(2,1)S(1)} %copy.28), channel_id=1, source_target_pairs={{2,0},{4,2},{6,4},{8,6},{10,8},{12,10},{14,12},{16,14},{18,16},{20... | collective-permute-start | bytes 786440 | tf_op jit(solution)/shard_map/ppermute | solution.py:18
  21.5 35.6 %copy-start.6 = (f32[2,128]{1,0:T(2,128)S(1)}, f32[2,128]{1,0:T(2,128)}, u32[]{:S(2)}) copy-start(f32[2,128]{1,0:T(2,128)} %param.19) | copy-start | bytes 3076
  56.2 1.2 copy-start.5
  56.2 3.0 copy-start.3
  1076.4 21.9 %copy-start.2 = (bf16[512,128]{1,0:T(8,128)(2,1)S(1)}, bf16[512,128]{1,0:T(8,128)(2,1)}, u32[]{:S(2)}) copy-start(bf16[512,128]{1,0:T(8,128)(2,1)} %param.13) | copy-start | bytes 393220
Sparse Core Ops, SparseCore 0:
  14.3 114.2 all-gather.2
  132.2 114.5 all-gather.4
  1074.0 24.2 reduce-scatter.1
where the time goes:
time: 1120 us; the launch traced here: 1110 us
  local copies, waits for them, and re-layouts  348 us (31%)
  other arithmetic  291 us (26%)
  waiting for transfers between devices  193 us (17%)
  loops' own time  164 us (15%)
  matrix products  88.2 us (8%)
  between operations  13.4 us (1%)
    reduce_max x128, other arithmetic, tile(): chosen_local = jnp.max(jnp.where(hit, local_of, -1))  169 us
    another operation x1, loops' own time, body(): lax.scan(advance, carry, jnp.arange(count // rows, dtype=jnp.int32))  164 us
    dynamic_slice x128, local copies, waits for them, and re-layouts, body(): lax.scan(advance, carry, jnp.arange(count // rows, dtype=jnp.int32))  155 us
    all_gather x1, waiting for transfers between devices, body(): key_piece = lax.all_gather(keys, 'blk', axis=0, tiled=True)  118 us
    dynamic_slice x256, local copies, waits for them, and re-layouts, tile(): block_keys = lax.dynamic_slice_in_dim(key_piece, begin, BLOCK, 0)  118 us
    reduce_or x128, other arithmetic, tile(): query_uses = jnp.any(hit, axis=1)  102 us
    dot_general x128, matrix products, tile(): jnp.einsum('qhd,khd->hqk', query_heads, block_keys.reshape(BLOCK, heads_h...  55.5 us
    all_gather x1, waiting for transfers between devices, body(): value_piece = lax.all_gather(values, 'blk', axis=0, tiled=True)  54.5 us
  transfers between devices with their start and end apart: 5, of which 3 were waited for; matrix products, arithmetic and copies ran while one was open for 5% of the time, Pallas kernels for 0%

commit v1 on v0

--- a/solution.py
+++ b/solution.py
@@ -5,6 +5,11 @@
 
 HEAD_DIM = 32
 BLOCK = 128
+
+
+def exchange_gather(value, axis, along):
+    sent = jnp.stack([value] * lax.axis_size(axis))
+    return jnp.concatenate(lax.all_to_all(sent, axis, 0, 0), axis=along)
 
 
 def padded(value, sides, width):
@@ -96,7 +101,7 @@
     initial = (jnp.zeros((rows, width), jnp.float32), jnp.zeros((heads_here, rows), jnp.float32))
     carry = initial
     key_piece = lax.all_gather(keys, "blk", axis=0, tiled=True)
-    value_piece = lax.all_gather(values, "blk", axis=0, tiled=True)
+    value_piece = exchange_gather(values, "blk", 0)
     count = key_piece.shape[0]
 
     def advance(state, turn):

time: 1120 us -> 1370 us (1.22)
  waiting for transfers between devices: 193 us -> 401 us
  local copies, waits for them, and re-layouts: 348 us -> 383 us
  other arithmetic: 291 us -> 275 us
  starting transfers between devices: 3.6 us -> 19.2 us
    all_to_all x0 -> x1, waiting for transfers between devices: none -> 317 us  [exchange_gather(): return jnp.concatenate(lax.all_to_all(sent, axis, 0, 0), axis=along)]
    all_gather x1, waiting for transfers between devices: 118 us -> 0.01 us  [body(): key_piece = lax.all_gather(keys, 'blk', axis=0, tiled=True)]
    all_gather x1 -> x0, waiting for transfers between devices: 54.5 us -> none  [body(): value_piece = lax.all_gather(values, 'blk', axis=0, tiled=True)]
    ppermute x1, waiting for transfers between devices: 0.01 us -> 47.1 us  [padded(): before = lax.ppermute(last, axis, up)]
    all_to_all x0 -> x1, local copies, waits for them, and re-layouts: none -> 21.9 us  [exchange_gather(): return jnp.concatenate(lax.all_to_all(sent, axis, 0, 0), axis=along)]
    all_to_all x0 -> x1, starting transfers between devices: none -> 17.4 us  [exchange_gather(): return jnp.concatenate(lax.all_to_all(sent, axis, 0, 0), axis=along)]
  transfers between devices with their start and end apart: 5 -> 5, of which waited for: 3 -> 4; matrix products, arithmetic and copies ran while one was open for 5% -> 6% of each run, Pallas kernels for 0% -> 0%
where the time goes in v1:
time: 1370 us; the launch traced here: 1350 us
  waiting for transfers between devices  401 us (29%)
  local copies, waits for them, and re-layouts  383 us (28%)
  other arithmetic  275 us (20%)
  loops' own time  170 us (12%)
  matrix products  86.9 us (6%)
  starting transfers between devices  19.2 us (1%)
    all_to_all x1, waiting for transfers between devices, exchange_gather(): return jnp.concatenate(lax.all_to_all(sent, axis, 0, 0), axis=along)  317 us
    another operation x1, loops' own time, body(): lax.scan(advance, carry, jnp.arange(count // rows, dtype=jnp.int32))  170 us
    dynamic_slice x128, local copies, waits for them, and re-layouts, body(): lax.scan(advance, carry, jnp.arange(count // rows, dtype=jnp.int32))  162 us
    reduce_max x128, other arithmetic, tile(): chosen_local = jnp.max(jnp.where(hit, local_of, -1))  161 us
    dynamic_slice x256, local copies, waits for them, and re-layouts, tile(): block_keys = lax.dynamic_slice_in_dim(key_piece, begin, BLOCK, 0)  118 us
    reduce_or x128, other arithmetic, tile(): query_uses = jnp.any(hit, axis=1)  95.2 us
    dot_general x128, matrix products, tile(): jnp.einsum('qhd,khd->hqk', query_heads, block_keys.reshape(BLOCK, heads_h...  55.7 us
    ppermute x1, waiting for transfers between devices, padded(): before = lax.ppermute(last, axis, up)  47.1 us
  transfers between devices with their start and end apart: 5, of which 4 were waited for; matrix products, arithmetic and copies ran while one was open for 6% of the time, Pallas kernels for 0%

profile of v1, /device:TPU:1, one launch (start us, length us, event | category | flops | bytes accessed | tf_op | source)
XLA Modules:
  0.0 1353.9 jit_solution(8704449814182419153)
XLA Ops:
  6.5 5.9 all_gather.6
  13.6 6.0 stack.2
  19.7 17.4 %all-to-all-start = ((bf16[128,512,128]{1,2,0:T(8,128)(2,1)}), bf16[128,512,128]{1,2,0:T(8,128)(2,1)}, u32[]{:S(2)}, u32[]{:S(2)}) async-start(bf16[128,512,128]{1,2,0:T(8,128)(2,1)} %stack.2), calls=%async_computation | async-start | bytes 33554432 | tf_op jit(solution)/shard_map/all_to_all | solution.py:12
  38.7 1.7 collective-permute-start
  40.9 34.6 %gather_fusion = s32[4096]{0:T(1024)S(1)} fusion(s32[4,4]{1,0:T(4,128)S(1)} %copy-done.1, s32[4096]{0:T(1024)S(1)} %reshape.122), kind=kCustom, calls=%fused_computation | custom fusion | bytes 65536 | tf_op jit(solution)/shard_map/gather | solution.py:61
  78.7 47.1 %collective-permute-done = bf16[512,256]{1,0:T(8,128)(2,1)S(1)} collective-permute-done((bf16[512,256]{1,0:T(8,128)(2,1)S(1)}, bf16[512,256]{1,0:T(8,128)(2,1)S(1)}, u32[]{:S(2)}, u32[]{:S(2)}) %collective-permute-start) | collective-permute-done | bytes 262176 | tf_op jit(solution)/shard_map/ppermute | solution.py:22
  125.9 10.8 collective-permute-done.1
  136.8 14.6 %gather_fusion.1 = bf16[4096,256]{1,0:T(8,128)(2,1)S(1)} fusion(bf16[1536,256]{1,0:T(8,128)(2,1)S(1)} %pad_maximum_fusion, s32[4096]{0:T(1024)S(1)} %broadcast_clamp_fusion), kind=kCustom, calls=%fused_computation.1 | custom fusion | bytes 4210688 | tf_op jit(solution)/shard_map/jit(_take)/gather | solution.py:64
  151.4 316.8 %all-to-all-done = bf16[128,512,128]{1,2,0:T(8,128)(2,1)} async-done(((bf16[128,512,128]{1,2,0:T(8,128)(2,1)}), bf16[128,512,128]{1,2,0:T(8,128)(2,1)}, u32[]{:S(2)}, u32[]{:S(2)}) %all-to-all-start) | async-done | bytes 16777248 | tf_op jit(solution)/shard_map/all_to_all | solution.py:12
  468.2 21.9 %copy.60 = bf16[128,512,128]{2,1,0:T(8,128)(2,1)} copy(bf16[128,512,128]{1,2,0:T(8,128)(2,1)} %all-to-all-done) | data formatting | bytes 33554432 | tf_op jit(solution)/shard_map/all_to_all | solution.py:12
  490.6 822.5 %while.15 = (s32[]{:T(128)}, f32[512,128]{0,1:T(8,128)S(1)}, f32[4,512]{1,0:T(4,128)S(1)}, s32[128]{0:T(128)}, s32[4,32]{1,0:T(4,128)}, /*index=5*/s32[4,32]{1,0...) while((s32[]{:T(128)}, f32[512,128]{0,1:T(8,128)S(1)}, ...), condition=%wide.region_5.6_spmd.clone, body=%wide.region_1.5_spmd.clone.sunk | while | flops 34736664 | bytes 2594593 | solution.py:113
  497.0 1.3 dynamic_slice.35
  503.4 1.3 dynamic_slice.35
  509.9 1.3 dynamic_slice.35
  516.3 1.3 dynamic_slice.35
  522.7 1.3 dynamic_slice.35
  529.1 1.3 dynamic_slice.35
  535.6 1.3 dynamic_slice.35
  548.4 1.3 dynamic_slice.35
  1313.1 1.9 fusion.38
  1315.0 2.5 convert_add_fusion
  1317.6 1.9 fusion.11
  1319.5 25.9 %reduce-scatter.2.cloned.1.call-done = f32[512,128]{1,0:T(8,128)} async-done(((f32[512,256]{1,0:T(8,128)}), f32[512,128]{1,0:T(8,128)}) %reduce-scatter.2.cloned.1.call-update) | async-done | bytes 262160 | tf_op jit(solution)/shard_map/reduce_scatter | solution.py:117
  1345.4 1.7 add_convert_fusion
  (1577 shorter events, 649.7 us)
Async XLA Ops:
  6.5 69.9 %copy-start = (bf16[2,256,128]{2,1,0:T(8,128)(2,1)S(1)}, bf16[2,256,128]{2,1,0:T(8,128)(2,1)}, u32[]{:S(2)}) copy-start(bf16[2,256,128]{2,1,0:T(8,128)(2,1)} %param.18) | copy-start | bytes 393220
  19.7 17.5 %copy-start.4 = (bf16[256,128]{1,0:T(8,128)(2,1)S(1)}, bf16[256,128]{1,0:T(8,128)(2,1)}, u32[]{:S(2)}) copy-start(bf16[256,128]{1,0:T(8,128)(2,1)} %param.15) | copy-start | bytes 196612
  19.7 18.4 %copy-start.3 = (bf16[2,256,128]{2,1,0:T(8,128)(2,1)S(1)}, bf16[2,256,128]{2,1,0:T(8,128)(2,1)}, u32[]{:S(2)}) copy-start(bf16[2,256,128]{2,1,0:T(8,128)(2,1)} %param.17) | copy-start | bytes 393220
  19.7 448.6 %all-to-all-start = ((bf16[128,512,128]{1,2,0:T(8,128)(2,1)}), bf16[128,512,128]{1,2,0:T(8,128)(2,1)}, u32[]{:S(2)}, u32[]{:S(2)}) async-start(bf16[128,512,128]{1,2,0:T(8,128)(2,1)} %stack.2), calls=%async_computation | async-start | bytes 33554432 | tf_op jit(solution)/shard_map/all_to_all | solution.py:12
  37.0 3.3 copy-start.6
  37.1 3.9 copy-start.1
  37.1 453.0 %all-gather.2.cloned.1.call-start = ((), (), s32[]{:S(2)}) async-start(), calls=%async_computation.2 | async-start | bytes 16908288 | tf_op jit(solution)/shard_map/all_gather | solution.py:103
  38.0 1307.3 %reduce-scatter.2.cloned.1.call-start = ((), (), s32[]{:S(2)}) async-start(), calls=%async_computation.3 | async-start | bytes 786432 | tf_op jit(solution)/shard_map/reduce_scatter | solution.py:117
  38.7 87.2 %collective-permute-start = (bf16[512,256]{1,0:T(8,128)(2,1)S(1)}, bf16[512,256]{1,0:T(8,128)(2,1)S(1)}, u32[]{:S(2)}, u32[]{:S(2)}) collective-permute-start(bf16[512,256]{1,0:T(8,128)(2,1)S(1)} %copy.54), channel_id=1, source_target_pairs={{0,2},{2,4},{4,6},{6,8},{8,10},{10,12},{12,14},{14,16},{16,18},{18... | collective-permute-start | bytes 786440 | tf_op jit(solution)/shard_map/ppermute | solution.py:22
  40.4 96.3 %collective-permute-start.1 = (bf16[512,256]{1,0:T(8,128)(2,1)S(1)}, bf16[512,256]{1,0:T(8,128)(2,1)S(1)}, u32[]{:S(2)}, u32[]{:S(2)}) collective-permute-start(bf16[512,256]{1,0:T(8,128)(2,1)S(1)} %copy.54), channel_id=1, source_target_pairs={{2,0},{4,2},{6,4},{8,6},{10,8},{12,10},{14,12},{16,14},{18,16},{20... | collective-permute-start | bytes 786440 | tf_op jit(solution)/shard_map/ppermute | solution.py:23
  40.9 35.6 %copy-start.8 = (f32[2,128]{1,0:T(2,128)S(1)}, f32[2,128]{1,0:T(2,128)}, u32[]{:S(2)}) copy-start(f32[2,128]{1,0:T(2,128)} %param.19) | copy-start | bytes 3076
  75.5 1.2 copy-start.7
  75.5 3.0 copy-start.5
  1317.6 27.8 %copy-start.2 = (bf16[512,128]{1,0:T(8,128)(2,1)S(1)}, bf16[512,128]{1,0:T(8,128)(2,1)}, u32[]{:S(2)}) copy-start(bf16[512,128]{1,0:T(8,128)(2,1)} %param.13) | copy-start | bytes 393220
Sparse Core Ops, SparseCore 0:
  41.5 315.6 all-gather.1
  1315.2 30.1 reduce-scatter.1
